TPU v7x, 256 devices: a whole 4x4x8 slice. The times are simulated.
256 devices in a mesh: seg: 8 (over x, core), blk: 32 (over z, y).
Axes of the slice: x: 4, y: 4, z: 8, core: 2. Of those that a mesh axis runs over, the one named last changes fastest.
Arguments:
- start_vector: bfloat16 [8, 128, 128, 128], P('seg', 'blk'), may hold values from -6 to 6
- left_environment: bfloat16 [8, 128, 34, 128, 128], P('seg', 'blk'), may hold values from -0.5 to 0.5
- right_environment: bfloat16 [8, 128, 34, 128, 128], P('seg', 'blk'), may hold values from -0.5 to 0.5
- block_energy: float32 [8, 128], P('seg', 'blk'), may hold values from -2 to 2
- sector_rows: int32 [8, 128], P('seg', 'blk'), may hold values from 32 to 128, as said below
- sector_cols: int32 [8, 128], P('seg', 'blk'), may hold values from 32 to 128, as said below
- feed_block: int32 [8, 128, 34], P('seg', 'blk'), may hold values from 0 to 128, as said below
Outputs:
- coefficients: float32 [8, 6], P('seg')
- residual: float32 [8, 128, 128, 128], P('seg', 'blk')
Inputs may be any that keep to these rules, and one draw needn't show every extreme that they name: `sector_rows`: the first block of every segment fills its tile. `sector_cols`: the first block of every segment fills its tile. `feed_block`: 128 marks an absent channel; absent channels come after the present ones of a block, and the first block of every segment has all 34 channels.
All inputs are finite; a program needn't handle non-finite values.
Results may differ from a plain program's by a relative error of at most 0.014.
Values may be sent and summed in bfloat16 or wider, within the bound.
A program may use at most 128 MiB of HBM per device.

v0:
```python
import jax
import jax.numpy as jnp
from jax import lax
from jax.sharding import PartitionSpec as P

STEPS = 3


epsilon = 1e-06


def passed_along(block, axis, distance):
    devices = range(lax.axis_size(axis))
    route = [(i - distance, i) for i in devices if i - distance in devices]
    return lax.ppermute(block, axis, route)


def local(
    start_vector,
    left_environment,
    right_environment,
    block_energy,
    sector_rows,
    sector_cols,
    feed_block,
):
    arrived = passed_along(left_environment, "seg", 1)
    left_tiles = arrived[0]
    right_tiles = right_environment[0]
    local_blocks = start_vector.shape[1]
    channels = left_environment.shape[2]
    tile_width = start_vector.shape[2]
    all_blocks = local_blocks * lax.axis_size("blk")
    own_index = lax.axis_index("blk")
    positions = jnp.arange(tile_width, dtype=jnp.int32)
    row_mask = (positions[None, :] < sector_rows[0][:, None]).astype(jnp.float32)
    col_mask = (positions[None, :] < sector_cols[0][:, None]).astype(jnp.float32)
    mask_tiles = row_mask[:, :, None] * col_mask[:, None, :]
    energy = block_energy[0]
    feeds = feed_block[0].reshape(local_blocks * channels)
    entries = float(all_blocks * tile_width * tile_width)
    vector = mask_tiles * start_vector[0].astype(jnp.float32)
    start_sum = lax.psum(jnp.sum(vector * vector), "blk")
    vector = vector * lax.rsqrt(start_sum / entries + epsilon)
    before = jnp.zeros_like(vector)
    coef_beta = jnp.float32(0.0)
    alphas = []
    betas = []
    image = vector
    for turn_index in range(STEPS):
        low_vector = vector.astype(jnp.bfloat16)
        half_product = jnp.einsum(
            "kwab,kbc->kwac", left_tiles, low_vector, preferred_element_type=jnp.float32
        ).astype(jnp.bfloat16)
        contrib = jnp.einsum(
            "kwac,kwcd->kwad", half_product, right_tiles, preferred_element_type=jnp.float32
        )
        contrib = contrib.reshape(local_blocks * channels, tile_width * tile_width)
        partial_value = jax.ops.segment_sum(contrib, feeds, num_segments=all_blocks + 1)
        partial_value = partial_value[:all_blocks].reshape(all_blocks, tile_width, tile_width)
        whole = lax.psum(partial_value.astype(jnp.bfloat16), "blk").astype(jnp.float32)
        summed = lax.dynamic_slice_in_dim(whole, own_index * local_blocks, local_blocks, 0)
        image = mask_tiles * summed + energy[:, None, None] * vector
        coef_alpha = lax.psum(jnp.sum(vector * image), "blk") / entries
        image = image - coef_alpha * vector - coef_beta * before
        mean_square = lax.psum(jnp.sum(image * image), "blk") / entries
        coef_beta = jnp.sqrt(mean_square)
        before = vector
        vector = image * lax.rsqrt(mean_square + epsilon)
        alphas.append(coef_alpha)
        betas.append(coef_beta)
    coefficients = jnp.stack(alphas + betas)[None, :]
    return (coefficients, image[None])


def solution(mesh):
    return jax.shard_map(
        local,
        mesh=mesh,
        in_specs=(
            P("seg", "blk", None, None),
            P("seg", "blk", None, None, None),
            P("seg", "blk", None, None, None),
            P("seg", "blk"),
            P("seg", "blk"),
            P("seg", "blk"),
            P("seg", "blk", None),
        ),
        out_specs=(P("seg", None), P("seg", "blk", None, None)),
        check_vma=False,
    )
```

profile of v0, /device:TPU:8, one launch (start us, length us, event | category | flops | bytes accessed | tf_op | source)
XLA Modules:
  0.0 1146.3 jit_solution(7200467232243111163)
XLA Ops:
  7.2 0.0 all-reduce.4.cloned.1.call-start
  7.2 3.8 collective-permute-start
  11.0 0.7 fusion.80
  11.8 1.6 fusion.58
  13.4 74.4 %psum.70 = f32[]{:T(128)} all-reduce(f32[]{:T(128)} %fusion.58), channel_id=1, replica_groups=mesh['seg'=8,'blk'=32] {'blk'}, use_global_device_ids=true, to_apply=%region_1.0 | all-reduce | flops 1 | bytes 8 | tf_op jit(solution)/shard_map/psum | solution.py:43
  87.8 0.8 reshape.74
  89.3 0.0 collective-permute-done
  89.3 9.6 fusion.15
  98.9 22.6 %scatter_custom_fusion = f32[129,16384]{1,0:T(8,128)} fusion(s32[136]{0:T(256)S(1)} %reshape.74, f32[17,8,128,128]{3,2,1,0:T(8,128)} %bitcast.114, f32[]{:T(128)} %constant.8.clone.1), kind=kCustom, calls=%fused_computation.9 | custom fusion | flops 2228224 | bytes 17367044 | tf_op jit(solution)/shard_map/scatter-add | solution.py:59
  121.5 4.1 fusion.30
  125.7 0.0 copy-start
  125.7 0.0 copy-start.1
  125.7 3.2 copy.13
  128.9 0.0 all-reduce.4.cloned.1.call-update
  128.9 0.4 all-reduce.6.cloned.1.call-start
  129.3 159.1 %all-reduce.4.cloned.1.call-done = bf16[128,128,128]{2,1,0:T(8,128)(2,1)} async-done(((bf16[128,128,128]{2,1,0:T(8,128)(2,1)}), bf16[128,128,128]{2,1,0:T(8,128)(2,1)}) %all-reduce.4.cloned.1.call-update) | async-done | bytes 4194320 | tf_op jit(solution)/shard_map/psum | solution.py:61
  288.4 0.0 copy-done
  288.4 0.0 copy-done.1
  288.4 1.7 fusion.55
  290.1 72.2 %psum.72 = f32[]{:T(128)} all-reduce(f32[]{:T(128)} %fusion.55), channel_id=1, replica_groups=mesh['seg'=8,'blk'=32] {'blk'}, use_global_device_ids=true, to_apply=%region_5.0 | all-reduce | flops 1 | bytes 8 | tf_op jit(solution)/shard_map/psum | solution.py:64
  362.9 1.7 multiply_reduce_fusion.4
  364.6 73.0 %psum.73 = f32[]{:T(128)} all-reduce(f32[]{:T(128)} %multiply_reduce_fusion.4), channel_id=1, replica_groups=mesh['seg'=8,'blk'=32] {'blk'}, use_global_device_ids=true, to_apply=%region_7.0 | all-reduce | flops 1 | bytes 8 | tf_op jit(solution)/shard_map/psum | solution.py:66
  438.4 9.7 fusion.11
  448.0 22.6 %scatter_custom_fusion.1 = f32[129,16384]{1,0:T(8,128)} fusion(s32[136]{0:T(256)S(1)} %reshape.74, f32[17,8,128,128]{3,2,1,0:T(8,128)} %bitcast.115, f32[]{:T(128)} %constant.8.clone.1), kind=kCustom, calls=%fused_computation.6 | custom fusion | flops 2228224 | bytes 17367044 | tf_op jit(solution)/shard_map/scatter-add | solution.py:59
  470.6 4.1 fusion.31
  474.7 3.2 copy.15
  478.0 0.0 all-reduce.6.cloned.1.call-update
  478.0 0.3 all-reduce.8.cloned.1.call-start
  478.3 159.8 %all-reduce.6.cloned.1.call-done = bf16[128,128,128]{2,1,0:T(8,128)(2,1)} async-done(((bf16[128,128,128]{2,1,0:T(8,128)(2,1)}), bf16[128,128,128]{2,1,0:T(8,128)(2,1)}) %all-reduce.6.cloned.1.call-update) | async-done | bytes 4194320 | tf_op jit(solution)/shard_map/psum | solution.py:61
  638.0 1.8 multiply_reduce_fusion.3
  639.9 72.2 %psum.75 = f32[]{:T(128)} all-reduce(f32[]{:T(128)} %multiply_reduce_fusion.3), channel_id=1, replica_groups=mesh['seg'=8,'blk'=32] {'blk'}, use_global_device_ids=true, to_apply=%region_11.0 | all-reduce | flops 1 | bytes 8 | tf_op jit(solution)/shard_map/psum | solution.py:64
  712.7 1.8 multiply_reduce_fusion.2
  714.6 73.0 %psum.76 = f32[]{:T(128)} all-reduce(f32[]{:T(128)} %get-tuple-element.4), channel_id=1, replica_groups=mesh['seg'=8,'blk'=32] {'blk'}, use_global_device_ids=true, to_apply=%region_13.0 | all-reduce | flops 1 | bytes 8 | tf_op jit(solution)/shard_map/psum | solution.py:66
  788.3 9.6 fusion.9
  797.9 22.6 %scatter_custom_fusion.2 = f32[129,16384]{1,0:T(8,128)} fusion(s32[136]{0:T(256)S(1)} %reshape.74, f32[17,8,128,128]{3,2,1,0:T(8,128)} %bitcast.113, f32[]{:T(128)} %constant.8.clone.1), kind=kCustom, calls=%fused_computation.3 | custom fusion | flops 2228224 | bytes 17367044 | tf_op jit(solution)/shard_map/scatter-add | solution.py:59
  820.5 4.1 fusion.32
  824.6 3.2 copy.17
  827.9 0.0 all-reduce.8.cloned.1.call-update
  827.9 160.0 %all-reduce.8.cloned.1.call-done = bf16[128,128,128]{2,1,0:T(8,128)(2,1)} async-done(((bf16[128,128,128]{2,1,0:T(8,128)(2,1)}), bf16[128,128,128]{2,1,0:T(8,128)(2,1)}) %all-reduce.8.cloned.1.call-update) | async-done | bytes 4194320 | tf_op jit(solution)/shard_map/psum | solution.py:61
  987.9 1.7 multiply_reduce_fusion.1
  989.6 72.2 %psum.78 = f32[]{:T(128)} all-reduce(f32[]{:T(128)} %multiply_reduce_fusion.1), channel_id=1, replica_groups=mesh['seg'=8,'blk'=32] {'blk'}, use_global_device_ids=true, to_apply=%region_17.0 | all-reduce | flops 1 | bytes 8 | tf_op jit(solution)/shard_map/psum | solution.py:64
  1062.4 2.5 multiply_reduce_fusion
  1065.0 73.0 %psum.79 = f32[]{:T(128)} all-reduce(f32[]{:T(128)} %get-tuple-element.2), channel_id=1, replica_groups=mesh['seg'=8,'blk'=32] {'blk'}, use_global_device_ids=true, to_apply=%region_19.0 | all-reduce | flops 1 | bytes 8 | tf_op jit(solution)/shard_map/psum | solution.py:66
  1138.7 0.6 stack.27
Async XLA Ops:
  7.2 281.3 %all-reduce.4.cloned.1.call-start = ((), (), s32[]{:S(2)}) async-start(), calls=%async_computation | async-start | bytes 8388608 | tf_op jit(solution)/shard_map/psum | solution.py:61
  7.2 82.1 %collective-permute-start = (bf16[1,4,34,128,128]{4,3,2,1,0:T(8,128)(2,1)}, bf16[1,4,34,128,128]{4,3,2,1,0:T(8,128)(2,1)}, u32[]{:S(2)}, u32[]{:S(2)}) collective-permute-start(bf16[1,4,34,128,128]{4,3,2,1,0:T(8,128)(2,1)} %param.8), channel_id=1, source_target_pairs={{0,32},{32,64},{64,96},{96,128},{128,160},{160,192},{192,224},{1,3... | collective-permute-start | bytes 13369352 | tf_op jit(solution)/shard_map/ppermute | solution.py:15
  125.7 162.8 %copy-start = (bf16[1,4,128,128]{3,2,1,0:T(8,128)(2,1)S(1)}, bf16[1,4,128,128]{3,2,1,0:T(8,128)(2,1)}, u32[]{:S(2)}) copy-start(bf16[1,4,128,128]{3,2,1,0:T(8,128)(2,1)} %param.7) | copy-start | bytes 393220
  125.7 162.7 %copy-start.1 = (f32[1,4]{1,0:T(1,128)S(1)}, f32[1,4]{1,0:T(1,128)}, u32[]{:S(2)}) copy-start(f32[1,4]{1,0:T(1,128)} %param.10) | copy-start | bytes 52
  128.9 509.1 %all-reduce.6.cloned.1.call-start = ((), (), s32[]{:S(2)}) async-start(), calls=%async_computation.1 | async-start | bytes 8388608 | tf_op jit(solution)/shard_map/psum | solution.py:61
  478.0 509.9 %all-reduce.8.cloned.1.call-start = ((), (), s32[]{:S(2)}) async-start(), calls=%async_computation.2 | async-start | bytes 8388608 | tf_op jit(solution)/shard_map/psum | solution.py:61
Sparse Core Ops, SparseCore 0:
  129.0 159.3 all-reduce.3
  478.1 159.8 all-reduce.5
  828.0 159.8 all-reduce.7
where the time goes:
time: 1150 us
  blocking collectives  510 us (44%)
  waiting for transfers between devices  479 us (42%)
  other arithmetic  81.4 us (7%)
  matrix products  28.9 us (3%)
  local copies, waits for them, and re-layouts  23.4 us (2%)
  between operations  19.1 us (2%)
    psum x3, waiting for transfers between devices, local(): lax.psum(partial_value.astype(jnp.bfloat16), 'blk').astype(jnp.float32)  479 us
    psum x3, blocking collectives, local(): mean_square = lax.psum(jnp.sum(image * image), 'blk') / entries  219 us
    psum x3, blocking collectives, local(): coef_alpha = lax.psum(jnp.sum(vector * image), 'blk') / entries  217 us
    psum x1, blocking collectives, local(): start_sum = lax.psum(jnp.sum(vector * vector), 'blk')  74.4 us
    scatter-add x3, other arithmetic, local(): jax.ops.segment_sum(contrib, feeds, num_segments=all_blocks + 1)  67.8 us
    dot_general x3, matrix products, local(): jnp.einsum('kwac,kwcd->kwad', half_product, right_tiles, preferred_elemen...  28.9 us
  transfers between devices with their start and end apart: 4, of which 3 were waited for; matrix products, arithmetic and copies ran while one was open for 0% of the time, Pallas kernels for 0%

commit v1 on v0

v1 whole, which is shorter than its diff:
```python
import functools

import jax
import jax.numpy as jnp
from jax import lax
from jax.experimental import pallas as pl
from jax.experimental.pallas import tpu as pltpu
from jax.sharding import PartitionSpec as P

STEPS = 3
EPS = 1e-06
T = 128
NK = 4
NW = 34
NS = NK * NW
NZ, NY = 8, 4
NBLK = NZ * NY
NSEG = 8
NT = NK * NBLK
PR = 32
NP = T // PR
ENTRIES = float(NT * T * T)
F32 = jnp.float32
BF16 = jnp.bfloat16
MESH = pl.DeviceIdType.MESH


def kernel(
    start_ref,
    left_ref,
    right_ref,
    energy_ref,
    rows_ref,
    cols_ref,
    order_ref,
    goal_ref,
    last_ref,
    has_ref,
    coef_ref,
    out_ref,
    lt,
    rt,
    half,
    run,
    qa,
    qb,
    sa,
    sb,
    ra,
    rb,
    rsa,
    rsb,
    cur,
    prev,
    img,
    low,
    coef,
    mine,
    xy,
    xz,
    lt_send,
    lt_recv,
    rt_sem,
    a1_send,
    a1_recv,
    a2_send,
    a2_recv,
    b1_send,
    b1_recv,
    b2_send,
    b2_recv,
    xy_send,
    xy_recv,
    xz_send,
    xz_recv,
):
    seg = lax.axis_index("seg")
    blk = lax.axis_index("blk")
    z = blk // NY
    y = blk % NY

    def at(dz=0, dy=0, ds=0):
        zz = lax.rem(z + dz + NZ, NZ)
        yy = lax.rem(y + dy + NY, NY)
        return (lax.rem(seg + ds + NSEG, NSEG), zz * NY + yy)

    barrier = pltpu.get_barrier_semaphore()
    peers = [at(dz=d) for d in range(1, NZ)] + [at(dy=d) for d in range(1, NY)]
    peers += [at(ds=1), at(ds=-1)]
    for peer in peers:
        pl.semaphore_signal(barrier, inc=1, device_id=peer, device_id_type=MESH)
    rt_copy = pltpu.make_async_copy(right_ref, rt, rt_sem)
    rt_copy.start()
    pl.semaphore_wait(barrier, len(peers))

    def lt_copy(j, k):
        return pltpu.make_async_remote_copy(
            src_ref=left_ref.at[k, :, pl.ds(j * PR, PR), :],
            dst_ref=lt.at[j, pl.ds(k * NW, NW)],
            send_sem=lt_send.at[j, k],
            recv_sem=lt_recv.at[j, k],
            device_id=at(ds=1),
            device_id_type=MESH,
        )

    for j in range(NP):
        for k in range(NK):
            lt_copy(j, k).start()

    def total(x):
        x = jnp.sum(x.reshape(NK * T, T), axis=0, keepdims=True)
        return jnp.broadcast_to(jnp.sum(x, axis=1, keepdims=True), (1, T))

    def merged(parts):
        dots = [p[0:1] for p in parts]
        sizes = [p[1:2] for p in parts]
        means = [p[2:3] for p in parts]
        rests = [p[3:4] for p in parts]
        dot, size, rest = sum(dots[1:], dots[0]), sum(sizes[1:], sizes[0]), sum(rests[1:], rests[0])
        weighted = [m * s for m, s in zip(means, sizes)]
        weighted = sum(weighted[1:], weighted[0])
        mean = jnp.where(size > 0.0, weighted / jnp.where(size > 0.0, size, 1.0), 0.0)
        spread = [s * (m - mean) * (m - mean) for m, s in zip(means, sizes)]
        return dot, size, mean, rest + sum(spread[1:], spread[0])

    def put(n, stage, own, values):
        for i, value in enumerate(values):
            mine[n, stage, pl.ds(i, 1), :] = value
        return mine[n, stage]

    def gathered(n, stage, size, me, box, sends, recvs, move):
        copies = []
        for d in range(1, size):
            copy = pltpu.make_async_remote_copy(
                src_ref=mine.at[n, stage],
                dst_ref=box.at[n, me],
                send_sem=sends.at[n, d],
                recv_sem=recvs.at[n, d],
                device_id=move(d),
                device_id_type=MESH,
            )
            copy.start()
            copies.append(copy)
        box[n, me] = mine[n, stage]
        for copy in copies:
            copy.wait()
        return merged([box[n, i] for i in range(size)])

    def exchange(n, values):
        put(n, 0, y, values)
        values = gathered(n, 0, NY, y, xy, xy_send, xy_recv, lambda d: at(dy=d))
        put(n, 1, z, values)
        return gathered(n, 1, NZ, z, xz, xz_send, xz_recv, lambda d: at(dz=d))

    row_at = lax.broadcasted_iota(jnp.int32, (T, T), 0)
    col_at = lax.broadcasted_iota(jnp.int32, (T, T), 1)

    def mask(tile, first, rows):
        live = (row_at[:rows] + first < rows_ref[tile]) & (col_at[:rows] < cols_ref[tile])
        return live

    for i in range(NK):
        cur[i] = jnp.where(mask(i, 0, T), start_ref[i].astype(F32), 0.0)
    zero = jnp.zeros((1, T), F32)
    _, size, _, _ = exchange(STEPS, (zero, total(cur[...] * cur[...]), zero, zero))
    scale = lax.rsqrt(size / ENTRIES + EPS)
    feeds_left = (seg > 0).astype(F32)
    for i in range(NK):
        q = cur[i] * scale
        cur[i] = q
        prev[i] = jnp.zeros((T, T), F32)
        low[i] = (q * feeds_left).astype(BF16)
    coef[...] = jnp.zeros((1, T), F32)

    def ring(buf, box, sends, recvs, n, me, move):
        far = n // 2

        def parts(up, d):
            if d < far:
                return pl.ds(0, 2)
            return pl.ds(0 if up else 1, 1)

        def copy(j, up, d):
            sign = 1 if up else -1
            goal = lax.rem(me + sign * d + n, n)
            return pltpu.make_async_remote_copy(
                src_ref=buf.at[j, goal, parts(up, d)],
                dst_ref=box.at[j, 0 if up else 1, d - 1, parts(up, d)],
                send_sem=sends.at[j, 0 if up else 1, d - 1],
                recv_sem=recvs.at[j, 0 if up else 1, d - 1],
                device_id=move(sign),
                device_id_type=MESH,
            )

        def step(j, hop):
            d = far - hop
            for up in (True, False):
                if hop > 0:
                    copy(j, up, d + 1).wait_recv()
                    goal = lax.rem(me + (d if up else -d) + n, n)
                    piece = parts(up, d + 1)
                    got = box[j, 0 if up else 1, d, piece].astype(F32)
                    buf[j, goal, piece] = (buf[j, goal, piece].astype(F32) + got).astype(BF16)
                copy(j, up, d).start()

        def last(j):
            copy(j, True, 1).wait_recv()
            copy(j, False, 1).wait_recv()

        def drain(j):
            for d in range(1, far + 1):
                copy(j, True, d).wait_send()
                copy(j, False, d).wait_send()

        return step, last, drain

    up_z = lambda s: at(dz=s)
    up_y = lambda s: at(dy=s)
    a1_step, a1_last, a1_drain = ring(qa, ra, a1_send, a1_recv, NZ, z, up_z)
    a2_step, a2_last, a2_drain = ring(sa, rsa, a2_send, a2_recv, NY, y, up_y)
    b1_step, b1_last, b1_drain = ring(qb, rb, b1_send, b1_recv, NY, y, up_y)
    b2_step, b2_last, b2_drain = ring(sb, rsb, b2_send, b2_recv, NZ, z, up_z)

    def a1_final(j):
        a1_last(j)
        for h in range(2):
            for i in range(NY):
                value = qa[j, z, h, i].astype(F32) + ra[j, 0, 0, h, i].astype(F32)
                sa[j, i, h] = (value + ra[j, 1, 0, h, i].astype(F32)).astype(BF16)

    def b1_final(j):
        b1_last(j)
        for h in range(2):
            for i in range(NZ):
                value = qb[j, y, h, i].astype(F32) + rb[j, 0, 0, h, i].astype(F32)
                sb[j, i, h] = (value + rb[j, 1, 0, h, i].astype(F32)).astype(BF16)

    def image(j, tile, value):
        rows = pl.ds(j * PR, PR)
        value = jnp.where(mask(tile, j * PR, PR), value, 0.0)
        img[tile, rows] = value + energy_ref[tile] * cur[tile, rows]

    def a2_final(j):
        a2_last(j)
        for h in range(2):
            value = sa[j, y, h].astype(F32) + rsa[j, 0, 0, h].astype(F32)
            image(j, h, value + rsa[j, 1, 0, h].astype(F32))

    def b2_final(j):
        b2_last(j)
        for h in range(2):
            value = sb[j, z, h].astype(F32) + rsb[j, 0, 0, h].astype(F32)
            image(j, 2 + h, value + rsb[j, 1, 0, h].astype(F32))

    def a_life(j):
        events = [functools.partial(a1_step, j, hop) for hop in range(NZ // 2)]

        def turn():
            a1_final(j)
            a2_step(j, 0)

        events.append(turn)
        events.append(functools.partial(a2_step, j, 1))
        events.append(functools.partial(a2_final, j))
        return events

    def b_life(j):
        events = [functools.partial(b1_step, j, hop) for hop in range(NY // 2)]

        def turn():
            b1_final(j)
            b2_step(j, 0)

        events.append(turn)
        events += [functools.partial(b2_step, j, hop) for hop in range(1, NZ // 2)]
        events.append(functools.partial(b2_final, j))
        return events

    LIFE = NZ // 2 + NY // 2 + 1

    def drain():
        for j in range(NP):
            a1_drain(j)
            a2_drain(j)
            b1_drain(j)
            b2_drain(j)

    CH = 17

    def contributions(first, count):
        rows = count * PR

        def left_body(i, carry):
            for c in range(count):
                for s in range(2):
                    slot = pl.multiple_of(i * CH, CH) + s * (2 * NW)
                    k = lax.div(i * CH, NW) + 2 * s
                    tiles = lt[first + c, pl.ds(slot, CH)].reshape(CH * PR, T)
                    value = jnp.dot(tiles, low[k], preferred_element_type=F32).astype(BF16)
                    half[pl.ds(slot, CH), pl.ds(c * PR, PR)] = value.reshape(CH, PR, T)
            return carry

        lax.fori_loop(0, NS // (2 * CH), left_body, 0)

        UN = 8

        def right_body(i, acc):
            values = []
            for n in range(UN):
                slot = order_ref[i * UN + n]
                values.append(
                    jnp.dot(half[slot, pl.ds(0, rows)], rt[slot], preferred_element_type=F32)
                )
            for n in range(UN):
                here = i * UN + n
                before = jnp.maximum(here - 1, 0)
                same = goal_ref[here] == goal_ref[before]
                acc = jnp.where(same, acc, 0.0) + values[n]
                run[here, pl.ds(0, rows)] = acc.astype(BF16)
            return acc

        lax.fori_loop(0, NS // UN, right_body, jnp.zeros((rows, T), F32))

        def pick(o, carry):
            zo, yo = lax.div(o, NY), lax.rem(o, NY)
            for tile in range(NK):
                t = o * NK + tile
                value = run[last_ref[t], pl.ds(0, rows)]
                value = jnp.where(has_ref[t] > 0, value, jnp.zeros_like(value))
                for c in range(count):
                    part = value[c * PR : (c + 1) * PR]
                    if tile < 2:
                        qa[first + c, zo, tile, yo] = part
                    else:
                        qb[first + c, yo, tile - 2, zo] = part
            return carry

        lax.fori_loop(0, NBLK, pick, 0)

    def finish(n, beta, last):
        q, u = cur[...], img[...]
        g = u - beta * prev[...]
        dot = total(q * u)
        size = total(q * q)
        along = total(q * g)
        mean = jnp.where(size > 0.0, along / jnp.where(size > 0.0, size, 1.0), 0.0)
        rest = g - mean * q
        rest = total(rest * rest)
        dot, size, mean, rest = exchange(n, (dot, size, mean, rest))
        alpha = dot / ENTRIES
        square = (rest + size * (mean - alpha) * (mean - alpha)) / ENTRIES
        new_beta = jnp.sqrt(square)
        scale = lax.rsqrt(square + EPS)
        lane = lax.broadcasted_iota(jnp.int32, (1, T), 1)
        value = jnp.where(lane == n, alpha, coef[...])
        coef[...] = jnp.where(lane == n + STEPS, new_beta, value)
        for i in range(NK):
            q = cur[i]
            u = img[i] - alpha * q - beta * prev[i]
            if last:
                out_ref[i] = u
            else:
                prev[i] = q
                u = u * scale
                cur[i] = u
                low[i] = (u * feeds_left).astype(BF16)
        return new_beta

    lives = [(a_life(j), b_life(j)) for j in range(NP)]

    def play(j, n):
        if 0 <= n < LIFE:
            for life in lives[j]:
                life[n]()

    rt_copy.wait()
    for turn in range(NP + LIFE - 1):
        if turn < NP:
            for k in range(NK):
                lt_copy(turn, k).wait_recv()
            contributions(turn, 1)
        for j in range(NP):
            play(j, turn - j)
    drain()
    for j in range(NP):
        for k in range(NK):
            lt_copy(j, k).wait_send()
    beta = finish(0, zero, False)

    for n in range(1, STEPS):
        contributions(0, 2)
        for j in (0, 1):
            play(j, 0)
        contributions(2, 2)
        for turn in range(1, LIFE + 1):
            for j in (0, 1):
                play(j, turn)
            for j in (2, 3):
                play(j, turn - 1)
        drain()
        beta = finish(n, beta, n == STEPS - 1)
    coef_ref[...] = coef[:, : 2 * STEPS]


def local(start, left, right, energy, rows, cols, feeds):
    feeds = feeds.reshape(NS)
    slots = jnp.arange(NS, dtype=jnp.int32)
    ahead = (feeds[None, :] < feeds[:, None]) | (
        (feeds[None, :] == feeds[:, None]) & (slots[None, :] < slots[:, None])
    )
    rank = jnp.sum(ahead.astype(jnp.int32), axis=1)
    here = rank[:, None] == slots[None, :]
    order = jnp.sum(jnp.where(here, slots[:, None], 0), axis=0)
    goal = jnp.sum(jnp.where(here, feeds[:, None], 0), axis=0)
    targets = jnp.arange(NT, dtype=jnp.int32)
    upto = jnp.sum((feeds[:, None] <= targets[None, :]).astype(jnp.int32), axis=0)
    has = jnp.sum((feeds[:, None] == targets[None, :]).astype(jnp.int32), axis=0)
    last = jnp.maximum(upto - 1, 0)

    vmem = pl.BlockSpec(memory_space=pltpu.VMEM)
    smem = pl.BlockSpec(memory_space=pltpu.SMEM)
    hbm = pl.BlockSpec(memory_space=pl.ANY)
    dma = pltpu.SemaphoreType.DMA
    coef, residual = pl.pallas_call(
        kernel,
        out_shape=(
            jax.ShapeDtypeStruct((1, 2 * STEPS), F32),
            jax.ShapeDtypeStruct((NK, T, T), F32),
        ),
        in_specs=[vmem, hbm, hbm] + [smem] * 7,
        out_specs=(vmem, vmem),
        scratch_shapes=[
            pltpu.VMEM((NP, NS, PR, T), BF16),
            pltpu.VMEM((NS, T, T), BF16),
            pltpu.VMEM((NS, 2 * PR, T), BF16),
            pltpu.VMEM((NS, 2 * PR, T), BF16),
            pltpu.VMEM((NP, NZ, 2, NY, PR, T), BF16),
            pltpu.VMEM((NP, NY, 2, NZ, PR, T), BF16),
            pltpu.VMEM((NP, NY, 2, PR, T), BF16),
            pltpu.VMEM((NP, NZ, 2, PR, T), BF16),
            pltpu.VMEM((NP, 2, NZ // 2, 2, NY, PR, T), BF16),
            pltpu.VMEM((NP, 2, NY // 2, 2, NZ, PR, T), BF16),
            pltpu.VMEM((NP, 2, NY // 2, 2, PR, T), BF16),
            pltpu.VMEM((NP, 2, NZ // 2, 2, PR, T), BF16),
            pltpu.VMEM((NK, T, T), F32),
            pltpu.VMEM((NK, T, T), F32),
            pltpu.VMEM((NK, T, T), F32),
            pltpu.VMEM((NK, T, T), BF16),
            pltpu.VMEM((1, T), F32),
            pltpu.VMEM((STEPS + 1, 2, 8, T), F32),
            pltpu.VMEM((STEPS + 1, NY, 8, T), F32),
            pltpu.VMEM((STEPS + 1, NZ, 8, T), F32),
            dma((NP, NK)),
            dma((NP, NK)),
            dma,
            dma((NP, 2, NZ // 2)),
            dma((NP, 2, NZ // 2)),
            dma((NP, 2, NY // 2)),
            dma((NP, 2, NY // 2)),
            dma((NP, 2, NY // 2)),
            dma((NP, 2, NY // 2)),
            dma((NP, 2, NZ // 2)),
            dma((NP, 2, NZ // 2)),
            dma((STEPS + 1, NY)),
            dma((STEPS + 1, NY)),
            dma((STEPS + 1, NZ)),
            dma((STEPS + 1, NZ)),
        ],
        compiler_params=pltpu.CompilerParams(
            collective_id=0, has_side_effects=True, vmem_limit_bytes=48 * 2**20
        ),
        cost_estimate=pl.CostEstimate(
            flops=STEPS * NS * 4 * T**3, bytes_accessed=4 * NS * T * T, transcendentals=0
        ),
        name="lanczos",
    )(
        start[0],
        left[0],
        right[0].reshape(NS, T, T),
        energy[0],
        rows[0],
        cols[0],
        order,
        goal,
        last,
        has,
    )
    return coef, residual[None]


def solution(mesh):
    return jax.shard_map(
        local,
        mesh=mesh,
        in_specs=(
            P("seg", "blk", None, None),
            P("seg", "blk", None, None, None),
            P("seg", "blk", None, None, None),
            P("seg", "blk"),
            P("seg", "blk"),
            P("seg", "blk"),
            P("seg", "blk", None),
        ),
        out_specs=(P("seg", None), P("seg", "blk", None, None)),
        check_vma=False,
    )
```

time: 1150 us -> 206 us (0.18)
  blocking collectives: 510 us -> 0 us
  waiting for transfers between devices: 479 us -> 0 us
  Pallas kernels: 0 us -> 197 us
  other arithmetic: 81.4 us -> 0.43 us
  matrix products: 28.9 us -> 0 us
  between operations: 19.1 us -> 0.66 us
  local copies, waits for them, and re-layouts: 23.4 us -> 7.1 us
    psum x7 -> x0, blocking collectives: 510 us -> none  [the longest x3 219 us: local(): mean_square = lax.psum(jnp.sum(image * image), 'blk') / entries]
    psum x3 -> x0, waiting for transfers between devices: 479 us -> none  [local(): lax.psum(partial_value.astype(jnp.bfloat16), 'blk').astype(jnp.float32)]
    pallas_call x0 -> x1, Pallas kernels: none -> 197 us  [local(): pl.pallas_call(kernel, out_shape=(jax.ShapeDtypeStruct((1, 2 * STEPS), F3...]
    scatter-add x3 -> x0, other arithmetic: 67.8 us -> none  [local(): jax.ops.segment_sum(contrib, feeds, num_segments=all_blocks + 1)]
    dot_general x3 -> x0, matrix products: 28.9 us -> none  [local(): jnp.einsum('kwac,kwcd->kwad', half_product, right_tiles, preferred_elemen...]
    unnamed x10 -> x12, local copies, waits for them, and re-layouts: 22 us -> 6.34 us
    reduce_sum x7 -> x3, other arithmetic: 12.8 us -> 0.42 us  [the longest x1 0.2 us: local(): rank = jnp.sum(ahead.astype(jnp.int32), axis=1)]
  transfers between devices with their start and end apart: 4 -> 0, of which waited for: 3 -> 0; matrix products, arithmetic and copies ran while one was open for 0% -> 0% of each run, Pallas kernels for 0% -> 0%
where the time goes in v1:
time: 206 us; the launch traced here: 205 us
  Pallas kernels  197 us (96%)
  local copies, waits for them, and re-layouts  7.1 us (3%)
    pallas_call x1, Pallas kernels, local(): pl.pallas_call(kernel, out_shape=(jax.ShapeDtypeStruct((1, 2 * STEPS), F3...  197 us
    unnamed x12, local copies, waits for them, and re-layouts  6.34 us

profile of v1, /device:TPU:8, one launch (start us, length us, event | category | flops | bytes accessed | tf_op | source)
XLA Modules:
  0.0 205.3 jit_solution(7917936191146102797)
XLA Ops:
  0.6 0.8 lt.32
  1.4 0.2 convert_reduce_fusion
  1.6 0.1 select_reduce_fusion
  1.7 0.1 convert_reduce_fusion.1
  1.8 0.0 copy-start
  1.8 2.3 %copy-done = bf16[1,4,34,128,128]{4,3,2,1,0:T(8,128)(2,1)S(1)} copy-done((bf16[1,4,34,128,128]{4,3,2,1,0:T(8,128)(2,1)S(1)}, bf16[1,4,34,128,128]{4,3,2,1,0:T(8,128)(2,1)}, u32[]{:S(2)}) %copy-start) | copy-done | bytes 4456472
  4.1 0.0 copy-start.1
  4.1 0.9 copy-done.1
  5.0 0.0 copy-start.2
  5.0 0.7 copy-done.2
  5.7 0.0 copy-start.3
  5.7 0.7 copy-done.3
  6.3 0.0 copy-start.4
  6.3 0.7 copy-done.4
  7.0 197.1 %lanczos.1 = (f32[1,6]{1,0:T(1,128)S(1)}, f32[4,128,128]{2,1,0:T(8,128)S(1)}) custom-call(bf16[4,128,128]{2,1,0:T(8,128)(2,1)S(1)} %bitcast.9, bf16[4,34,128,128]{3,2,1,0:T(8,128)(2,1)S(1)} %bitcast.8, bf16[136,128,128]{2,1,0:T(8,128)(2,1)} %bitcast.13, f32[4]{0:T(128)S(1)} %bitcast.10, s32[4]{0:T(128)S(1)} %bitcast.11, s32[4]{0:T(128)S(1)} %bitcast.12, ...), custom_call_target="tpu_custom_call" | custom-call | flops 3422552064 | bytes 8912896 | tf_op jit(solution)/shard_map/lanczos/pallas_call | solution.py:424
  204.1 0.5 copy.11
  204.6 0.7 copy.12
  (1 shorter events, 0.0 us)
Async XLA Ops:
  1.8 2.3 %copy-start = (bf16[1,4,34,128,128]{4,3,2,1,0:T(8,128)(2,1)S(1)}, bf16[1,4,34,128,128]{4,3,2,1,0:T(8,128)(2,1)}, u32[]{:S(2)}) copy-start(bf16[1,4,34,128,128]{4,3,2,1,0:T(8,128)(2,1)} %param.8) | copy-start | bytes 13369348
  4.1 0.9 copy-start.1
  5.0 0.7 copy-start.2
  5.7 0.7 copy-start.3
  6.3 0.7 copy-start.4

commit v2 on v1

v2 whole, which is shorter than its diff:
```python
import functools

import jax
import jax.numpy as jnp
from jax import lax
from jax.experimental import pallas as pl
from jax.experimental.pallas import tpu as pltpu
from jax.sharding import PartitionSpec as P

STEPS = 3
EPS = 1e-06
T = 128
NK = 4
NW = 34
NS = NK * NW
NZ, NY = 8, 4
NBLK = NZ * NY
NSEG = 8
NT = NK * NBLK
PR = 32
NP = T // PR
HR = PR // 2
NA = (2, 2, 1, 1)
A2_DIRECT = (True,) * NP
B2_ROUNDS = (2, 2, 2, 2)
ENTRIES = float(NT * T * T)
F32 = jnp.float32
BF16 = jnp.bfloat16
MESH = pl.DeviceIdType.MESH


def kernel(
    start_hbm,
    left_ref,
    right_ref,
    energy_hbm,
    rows_hbm,
    cols_hbm,
    order_hbm,
    goal_hbm,
    last_hbm,
    has_hbm,
    coef_ref,
    out_ref,
    start_ref,
    scalars,
    scalar_sem,
    lt,
    rt,
    half,
    run,
    qa,
    qb,
    sa,
    sb,
    ra,
    rb,
    rsa,
    rsb,
    cur,
    prev,
    img,
    near,
    ahead,
    low,
    coef,
    mine,
    xy,
    xz,
    lt_send,
    lt_recv,
    rt_sem,
    a1_send,
    a1_recv,
    a2_send,
    a2_recv,
    b1_send,
    b1_recv,
    b2_send,
    b2_recv,
    xy_send,
    xy_recv,
    xz_send,
    xz_recv,
):
    seg = lax.axis_index("seg")
    blk = lax.axis_index("blk")
    z = blk // NY
    y = blk % NY

    def at(dz=0, dy=0, ds=0):
        zz = lax.rem(z + dz + NZ, NZ)
        yy = lax.rem(y + dy + NY, NY)
        return (lax.rem(seg + ds + NSEG, NSEG), zz * NY + yy)

    barrier = pltpu.get_barrier_semaphore()
    peers = [at(ds=1), at(ds=-1)]
    peers += [at(dz=d) for d in (4, 3, 5, 2, 6, 1, 7)] + [at(dy=d) for d in (2, 1, 3)]
    for peer in peers:
        pl.semaphore_signal(barrier, inc=1, device_id=peer, device_id_type=MESH)
    energy_ref, rows_ref, cols_ref, order_ref, goal_ref, last_ref, has_ref = scalars
    local_copies = [pltpu.make_async_copy(start_hbm, start_ref, scalar_sem.at[7])]
    sources = (energy_hbm, rows_hbm, cols_hbm, order_hbm, goal_hbm, last_hbm, has_hbm)
    for i, (source, goal) in enumerate(zip(sources, scalars)):
        local_copies.append(pltpu.make_async_copy(source, goal, scalar_sem.at[i]))
    local_copies.append(pltpu.make_async_copy(right_ref, rt, rt_sem))
    for copy in local_copies:
        copy.start()
    pl.semaphore_wait(barrier, len(peers))

    def lt_copy(j, k):
        return pltpu.make_async_remote_copy(
            src_ref=left_ref.at[k, :, pl.ds(j * PR, PR), :],
            dst_ref=lt.at[j, pl.ds(k * NW, NW)],
            send_sem=lt_send.at[j, k],
            recv_sem=lt_recv.at[j, k],
            device_id=at(ds=1),
            device_id_type=MESH,
        )

    for j in range(NP):
        for k in range(NK):
            lt_copy(j, k).start()
    for copy in local_copies:
        copy.wait()

    def total(parts):
        x = sum(parts[1:], parts[0])
        x = jnp.sum(x, axis=0, keepdims=True)
        return jnp.broadcast_to(jnp.sum(x, axis=1, keepdims=True), (1, T))

    def merged(parts):
        rows = [[p[i : i + 1] for p in parts] for i in range(7)]
        add = lambda values: sum(values[1:], values[0])
        sizes, means = rows[1], rows[2]
        size = add(sizes)
        weighted = add([m * s for m, s in zip(means, sizes)])
        mean = jnp.where(size > 0.0, weighted / jnp.where(size > 0.0, size, 1.0), 0.0)
        spread = add([s * (m - mean) * (m - mean) for m, s in zip(means, sizes)])
        return [add(rows[0]), size, mean, add(rows[3]) + spread] + [add(r) for r in rows[4:]]

    def copies_of(n, stage, size, me, box, sends, recvs, move, order):
        return [
            pltpu.make_async_remote_copy(
                src_ref=mine.at[n, stage],
                dst_ref=box.at[n, me],
                send_sem=sends.at[n, d],
                recv_sem=recvs.at[n, d],
                device_id=move(d),
                device_id_type=MESH,
            )
            for d in order
        ]

    def stage_y(n):
        return copies_of(n, 0, NY, y, xy, xy_send, xy_recv, lambda d: at(dy=d), (2, 1, 3))

    def stage_z(n):
        order = (4, 3, 5, 2, 6, 1, 7)
        return copies_of(n, 1, NZ, z, xz, xz_send, xz_recv, lambda d: at(dz=d), order)

    def post(n, stage, values, copies, box, me):
        for i, value in enumerate(values):
            mine[n, stage, pl.ds(i, 1), :] = value
        for copy in copies:
            copy.start()
        box[n, me] = mine[n, stage]

    def exchange_open(n, values):
        post(n, 0, values, stage_y(n), xy, y)

    def exchange_pass(n):
        for copy in stage_y(n):
            copy.wait()
        post(n, 1, merged([xy[n, i] for i in range(NY)]), stage_z(n), xz, z)

    def exchange_close(n):
        for copy in stage_z(n):
            copy.wait()
        return merged([xz[n, i] for i in range(NZ)])

    row_at = lax.broadcasted_iota(jnp.int32, (T, T), 0)
    col_at = lax.broadcasted_iota(jnp.int32, (T, T), 1)

    def mask(tile, first, rows):
        return (row_at[:rows] + first < rows_ref[tile]) & (col_at[:rows] < cols_ref[tile])

    def mean_energy(weighted, size):
        value = jnp.where(size > 0.0, weighted / jnp.where(size > 0.0, size, 1.0), 0.0)
        return jnp.clip(value, -2.0, 2.0)

    zero = jnp.zeros((1, T), F32)
    squares = []
    for i in range(NK):
        q = jnp.where(mask(i, 0, T), start_ref[i].astype(F32), 0.0)
        cur[i] = q
        squares.append(q * q)
    weighted = total([square * energy_ref[i] for i, square in enumerate(squares)])
    exchange_open(STEPS, [zero, total(squares), zero, zero, weighted, zero, zero])
    exchange_pass(STEPS)
    _, size, _, _, weighted, _, _ = exchange_close(STEPS)
    scale = lax.rsqrt(size / ENTRIES + EPS)
    shift = mean_energy(weighted, size)
    feeds_left = (seg > 0).astype(F32)
    for i in range(NK):
        q = cur[i] * scale
        cur[i] = q
        prev[i] = jnp.zeros((T, T), F32)
        near[i] = jnp.zeros((T, T), F32)
        low[i] = (q * feeds_left).astype(BF16)
    coef[...] = jnp.zeros((1, T), F32)

    def ring(side, bufs, boxes, sends, recvs, n, me, move):
        far = n // 2

        def parts(up, d):
            if d < far:
                return pl.ds(0, 2)
            return pl.ds(0 if up else 1, 1)

        def copy(j, up, d):
            sign = 1 if up else -1
            goal = lax.rem(me + sign * d + n, n)
            return pltpu.make_async_remote_copy(
                src_ref=bufs[j].at[goal, parts(up, d)],
                dst_ref=boxes[j].at[side, 0 if up else 1, d - 1, parts(up, d)],
                send_sem=sends.at[side * NP + j, 0 if up else 1, d - 1],
                recv_sem=recvs.at[side * NP + j, 0 if up else 1, d - 1],
                device_id=move(sign),
                device_id_type=MESH,
            )

        def step(j, hop):
            d = far - hop
            for up in (True, False):
                if hop > 0:
                    copy(j, up, d + 1).wait_recv()
                    goal = lax.rem(me + (d if up else -d) + n, n)
                    piece = parts(up, d + 1)
                    got = boxes[j][side, 0 if up else 1, d, piece].astype(F32)
                    own = bufs[j][goal, piece].astype(F32)
                    bufs[j][goal, piece] = (own + got).astype(BF16)
                copy(j, up, d).start()

        def last(j, h):
            return [boxes[j][side, i, 0, h] for i in range(2)]

        def arrive(j):
            copy(j, True, 1).wait_recv()
            copy(j, False, 1).wait_recv()

        def drain(j):
            for d in range(1, far + 1):
                copy(j, True, d).wait_send()
                copy(j, False, d).wait_send()

        return step, arrive, last, drain

    def direct(side, bufs, boxes, sends, recvs, n, me, move):
        far = n // 2
        order = sorted(range(1, n), key=lambda d: -min(d, n - d))

        def copy(j, d):
            at_box = ((d - 1) // far, (d - 1) % far)
            return pltpu.make_async_remote_copy(
                src_ref=bufs[j].at[lax.rem(me + d, n)],
                dst_ref=boxes[j].at[(side,) + at_box],
                send_sem=sends.at[(side * NP + j,) + at_box],
                recv_sem=recvs.at[(side * NP + j,) + at_box],
                device_id=move(d),
                device_id_type=MESH,
            )

        def step(j, hop):
            for d in order:
                copy(j, d).start()

        def arrive(j):
            for d in order:
                copy(j, d).wait_recv()

        def last(j, h):
            return [boxes[j][side, (d - 1) // far, (d - 1) % far, h] for d in range(1, n)]

        def drain(j):
            for d in order:
                copy(j, d).wait_send()

        return step, arrive, last, drain

    def relay(side, bufs, boxes, sends, recvs, n, me, move):
        far = n // 2
        rounds = [(up, d) for d in range(far, 0, -1) for up in (True, False)]

        def parts(up, d):
            if d < far:
                return pl.ds(0, 2)
            return pl.ds(0 if up else 1, 1)

        def copy(j, up, d):
            sign = 1 if up else -1
            row = 0 if up else 1
            return pltpu.make_async_remote_copy(
                src_ref=bufs[j].at[lax.rem(me + sign * d + n, n), parts(up, d)],
                dst_ref=boxes[j].at[side, row, d - 1, parts(up, d)],
                send_sem=sends.at[side * NP + j, row, d - 1],
                recv_sem=recvs.at[side * NP + j, row, d - 1],
                device_id=move(sign * max(d - 1, 1)),
                device_id_type=MESH,
            )

        def step(j, hop):
            if hop == 0:
                for up, d in rounds[:-2]:
                    copy(j, up, d).start()
                return
            for up, d in rounds[:-2]:
                copy(j, up, d).wait_recv()
            for up in (True, False):
                row = 0 if up else 1
                goal = lax.rem(me + (1 if up else -1) + n, n)
                for h in range(2):
                    reach = range(2, far + 1 if h == row else far)
                    terms = [boxes[j][side, row, d - 1, h] for d in reach]
                    bufs[j][goal, h] = add([bufs[j][goal, h]] + terms).astype(BF16)
                copy(j, up, 1).start()

        def arrive(j):
            copy(j, True, 1).wait_recv()
            copy(j, False, 1).wait_recv()

        def last(j, h):
            return [boxes[j][side, i, 0, h] for i in range(2)]

        def drain(j):
            for up, d in rounds:
                copy(j, up, d).wait_send()

        return step, arrive, last, drain

    up_z = lambda s: at(dz=s)
    up_y = lambda s: at(dy=s)
    def add(values):
        values = [value.astype(F32) for value in values]
        return sum(values[1:], values[0])

    def turn_over(j, stage, src, me, goals, count, wide):
        _, arrive, last, _ = stage
        arrive(j)
        for h in range(2):
            got = last(j, h)
            for c in range(count):
                for i in range(wide):
                    value = add([src[j][me, h, c, i]] + [g[c, i] for g in got])
                    goals[j][i, h, c] = value.astype(BF16)

    def image(j, tile, h, value):
        first = j * PR + h * HR
        img[tile, pl.ds(first, HR)] = jnp.where(mask(tile, first, HR), value, 0.0)

    def into_image(j, stage, src, me, count, first_tile):
        _, arrive, last, _ = stage
        arrive(j)
        for h in range(2):
            got = last(j, h)
            for c in range(count):
                image(j, first_tile + c, h, add([src[j][me, h, c]] + [g[c] for g in got]))

    def network(side):
        a1 = ring(side, qa, ra, a1_send, a1_recv, NZ, z, up_z)
        b1 = ring(side, qb, rb, b1_send, b1_recv, NY, y, up_y)
        a2_args = (side, sa, rsa, a2_send, a2_recv, NY, y, up_y)
        b2_args = (side, sb, rsb, b2_send, b2_recv, NZ, z, up_z)
        a2_of = [(direct if flag else ring)(*a2_args) for flag in A2_DIRECT]
        b2_of = [{1: direct, 2: relay, 4: ring}[r](*b2_args) for r in B2_ROUNDS]

        def a_life(j):
            events = [functools.partial(a1[0], j, hop) for hop in range(NZ // 2)]

            def turn():
                turn_over(j, a1, qa, z, sa, NA[j], NY)
                a2_of[j][0](j, 0)

            events.append(turn)
            if not A2_DIRECT[j]:
                events += [functools.partial(a2_of[j][0], j, hop) for hop in range(1, NY // 2)]
            events.append(lambda: into_image(j, a2_of[j], sa, y, NA[j], 0))
            return events

        def b_life(j):
            events = [functools.partial(b1[0], j, hop) for hop in range(NY // 2)]

            def turn():
                turn_over(j, b1, qb, y, sb, NK - NA[j], NZ)
                b2_of[j][0](j, 0)

            events.append(turn)
            events += [functools.partial(b2_of[j][0], j, hop) for hop in range(1, B2_ROUNDS[j])]
            events.append(lambda: into_image(j, b2_of[j], sb, z, NK - NA[j], NA[j]))
            return events

        lives = [(a_life(j), b_life(j)) for j in range(NP)]
        life_of = [max(len(a), len(b)) for a, b in lives]

        def play(j, n):
            for life in lives[j]:
                if 0 <= n < len(life):
                    life[n]()

        def drain():
            for j in range(NP):
                for stage in (a1, b1, a2_of[j], b2_of[j]):
                    stage[3](j)

        return play, drain, max(life_of)

    networks = [network(0), network(1)]

    CH = 17
    UN = 8

    def contributions(first, count):
        rows = count * PR

        def left_body(i, carry):
            for c in range(count):
                for s in range(2):
                    slot = pl.multiple_of(i * CH, CH) + s * (2 * NW)
                    k = lax.div(i * CH, NW) + 2 * s
                    tiles = lt[first + c, pl.ds(slot, CH)].reshape(CH * PR, T)
                    value = jnp.dot(tiles, low[k], preferred_element_type=F32).astype(BF16)
                    half[pl.ds(slot, CH), pl.ds(c * PR, PR)] = value.reshape(CH, PR, T)
            return carry

        lax.fori_loop(0, NS // (2 * CH), left_body, 0)

        def right_body(i, acc):
            values = []
            for n in range(UN):
                slot = order_ref[i * UN + n]
                values.append(
                    jnp.dot(half[slot, pl.ds(0, rows)], rt[slot], preferred_element_type=F32)
                )
            for n in range(UN):
                here = i * UN + n
                before = jnp.maximum(here - 1, 0)
                same = goal_ref[here] == goal_ref[before]
                acc = jnp.where(same, acc, 0.0) + values[n]
                run[here, pl.ds(0, rows)] = acc.astype(BF16)
            return acc

        lax.fori_loop(0, NS // UN, right_body, jnp.zeros((rows, T), F32))

        def pick(o, carry):
            zo, yo = lax.div(o, NY), lax.rem(o, NY)
            for tile in range(NK):
                t = o * NK + tile
                value = run[last_ref[t], pl.ds(0, rows)]
                value = jnp.where(has_ref[t] > 0, value, jnp.zeros_like(value))
                for c in range(count):
                    for h in range(2):
                        part = value[c * PR + h * HR : c * PR + (h + 1) * HR]
                        j = first + c
                        if tile < NA[j]:
                            qa[j][zo, h, tile, yo] = part
                        else:
                            qb[j][yo, h, tile - NA[j], zo] = part
            return carry

        lax.fori_loop(0, NBLK, pick, 0)

    def settle(extra, scale, beta, shift):
        for i in range(NK):
            n_q = img[i]
            if scale is not None:
                n_q = (n_q - extra * near[i]) * scale
            near[i] = n_q
            g = n_q + (energy_ref[i] - shift) * cur[i] - beta * prev[i]
            ahead[i] = g
            low[i] = (g * feeds_left).astype(BF16)

    def sums(shift):
        dots, sizes, alongs, ones, twos, threes = [], [], [], [], [], []
        for i in range(NK):
            q, w, e = cur[i], ahead[i], energy_ref[i]
            dots.append(q * (near[i] + e * q))
            sizes.append(q * q)
            alongs.append(q * w)
            ones.append(e * (w * w))
            twos.append(e * (w * q))
            threes.append(e * (q * q))
        size, along = total(sizes), total(alongs)
        mean = jnp.where(size > 0.0, along / jnp.where(size > 0.0, size, 1.0), 0.0)
        rests = []
        for i in range(NK):
            rest = ahead[i] - mean * cur[i]
            rests.append(rest * rest)
        return [
            total(dots), size, mean, total(rests), total(ones), total(twos), total(threes),
        ]

    def conclude(n, shift):
        dot, size, mean, rest, one, two, three = exchange_close(n)
        alpha = dot / ENTRIES
        extra = alpha - shift
        whole = rest + size * (mean - extra) * (mean - extra)
        square = whole / ENTRIES
        beta = jnp.sqrt(square)
        lane = lax.broadcasted_iota(jnp.int32, (1, T), 1)
        value = jnp.where(lane == n, alpha, coef[...])
        coef[...] = jnp.where(lane == n + STEPS, beta, value)
        next_shift = mean_energy(one - 2.0 * extra * two + extra * extra * three, whole)
        return extra, lax.rsqrt(square + EPS), beta, next_shift

    play, drain, turns = networks[0]
    for j in range(NP):
        for i in range(j):
            play(i, 2 * (j - i) - 1)
        for k in range(NK):
            lt_copy(j, k).wait_recv()
        contributions(j, 1)
        for i in range(j + 1):
            play(i, 2 * (j - i))
    for turn in range(1, turns):
        for j in range(NP):
            play(j, 2 * (NP - 1 - j) + turn)
    drain()
    for j in range(NP):
        for k in range(NK):
            lt_copy(j, k).wait_send()
    settle(None, None, zero, shift)

    for n in range(1, STEPS):
        play, drain, turns = networks[n % 2]
        contributions(0, NP)
        for j in range(NP):
            play(j, 0)
        exchange_open(n - 1, sums(shift))
        extra = scale = beta = None
        for turn in range(1, turns):
            for j in range(NP):
                play(j, turn)
            if turn == 1:
                exchange_pass(n - 1)
            if turn == 3:
                extra, scale, beta, next_shift = conclude(n - 1, shift)
                shift = next_shift
                for i in range(NK):
                    q = cur[i]
                    prev[i] = q
                    cur[i] = (ahead[i] - extra * q) * scale
        drain()
        settle(extra, scale, beta, shift)
    exchange_open(STEPS - 1, sums(shift))
    exchange_pass(STEPS - 1)
    extra, _, _, _ = conclude(STEPS - 1, shift)
    for i in range(NK):
        out_ref[i] = ahead[i] - extra * cur[i]
    coef_ref[...] = coef[:, : 2 * STEPS]


def local(start, left, right, energy, rows, cols, feeds):
    feeds = feeds.reshape(NS)
    slots = jnp.arange(NS, dtype=jnp.int32)
    ahead = (feeds[None, :] < feeds[:, None]) | (
        (feeds[None, :] == feeds[:, None]) & (slots[None, :] < slots[:, None])
    )
    rank = jnp.sum(ahead.astype(jnp.int32), axis=1)
    here = rank[:, None] == slots[None, :]
    order = jnp.sum(jnp.where(here, slots[:, None], 0), axis=0)
    goal = jnp.sum(jnp.where(here, feeds[:, None], 0), axis=0)
    targets = jnp.arange(NT, dtype=jnp.int32)
    upto = jnp.sum((feeds[:, None] <= targets[None, :]).astype(jnp.int32), axis=0)
    has = jnp.sum((feeds[:, None] == targets[None, :]).astype(jnp.int32), axis=0)
    last = jnp.maximum(upto - 1, 0)

    vmem = pl.BlockSpec(memory_space=pltpu.VMEM)
    hbm = pl.BlockSpec(memory_space=pl.ANY)
    dma = pltpu.SemaphoreType.DMA

    def piecewise(shape):
        return [pltpu.VMEM(shape(na, NK - na), BF16) for na in NA]

    coef, residual = pl.pallas_call(
        kernel,
        out_shape=(
            jax.ShapeDtypeStruct((1, 2 * STEPS), F32),
            jax.ShapeDtypeStruct((NK, T, T), F32),
        ),
        in_specs=[hbm] * 10,
        out_specs=(vmem, vmem),
        scratch_shapes=[
            pltpu.VMEM((NK, T, T), BF16),
            [pltpu.SMEM((NK,), F32)]
            + [pltpu.SMEM((size,), jnp.int32) for size in (NK, NK, NS, NS, NT, NT)],
            dma((8,)),
            pltpu.VMEM((NP, NS, PR, T), BF16),
            pltpu.VMEM((NS, T, T), BF16),
            pltpu.VMEM((NS, T, T), BF16),
            pltpu.VMEM((NS, T, T), BF16),
            piecewise(lambda na, nb: (NZ, 2, na, NY, HR, T)),
            piecewise(lambda na, nb: (NY, 2, nb, NZ, HR, T)),
            piecewise(lambda na, nb: (NY, 2, na, HR, T)),
            piecewise(lambda na, nb: (NZ, 2, nb, HR, T)),
            piecewise(lambda na, nb: (2, 2, NZ // 2, 2, na, NY, HR, T)),
            piecewise(lambda na, nb: (2, 2, NY // 2, 2, nb, NZ, HR, T)),
            piecewise(lambda na, nb: (2, 2, NY // 2, 2, na, HR, T)),
            piecewise(lambda na, nb: (2, 2, NZ // 2, 2, nb, HR, T)),
            pltpu.VMEM((NK, T, T), F32),
            pltpu.VMEM((NK, T, T), F32),
            pltpu.VMEM((NK, T, T), F32),
            pltpu.VMEM((NK, T, T), F32),
            pltpu.VMEM((NK, T, T), F32),
            pltpu.VMEM((NK, T, T), BF16),
            pltpu.VMEM((1, T), F32),
            pltpu.VMEM((STEPS + 1, 2, 8, T), F32),
            pltpu.VMEM((STEPS + 1, NY, 8, T), F32),
            pltpu.VMEM((STEPS + 1, NZ, 8, T), F32),
            dma((NP, NK)),
            dma((NP, NK)),
            dma,
            dma((2 * NP, 2, NZ // 2)),
            dma((2 * NP, 2, NZ // 2)),
            dma((2 * NP, 2, NY // 2)),
            dma((2 * NP, 2, NY // 2)),
            dma((2 * NP, 2, NY // 2)),
            dma((2 * NP, 2, NY // 2)),
            dma((2 * NP, 2, NZ // 2)),
            dma((2 * NP, 2, NZ // 2)),
            dma((STEPS + 1, NY)),
            dma((STEPS + 1, NY)),
            dma((STEPS + 1, NZ)),
            dma((STEPS + 1, NZ)),
        ],
        compiler_params=pltpu.CompilerParams(
            collective_id=0, has_side_effects=True, vmem_limit_bytes=60 * 2**20
        ),
        cost_estimate=pl.CostEstimate(
            flops=STEPS * NS * 4 * T**3, bytes_accessed=4 * NS * T * T, transcendentals=0
        ),
        name="lanczos",
    )(
        start[0],
        left[0],
        right[0].reshape(NS, T, T),
        energy[0],
        rows[0],
        cols[0],
        order,
        goal,
        last,
        has,
    )
    return coef, residual[None]


def solution(mesh):
    return jax.shard_map(
        local,
        mesh=mesh,
        in_specs=(
            P("seg", "blk", None, None),
            P("seg", "blk", None, None, None),
            P("seg", "blk", None, None, None),
            P("seg", "blk"),
            P("seg", "blk"),
            P("seg", "blk"),
            P("seg", "blk", None),
        ),
        out_specs=(P("seg", None), P("seg", "blk", None, None)),
        check_vma=False,
    )
```

time: 206 us -> 172 us (0.83)
  Pallas kernels: 197 us -> 165 us
  local copies, waits for them, and re-layouts: 7.1 us -> 3.52 us
    pallas_call x1, Pallas kernels: 197 us -> 165 us  [local(): pl.pallas_call(kernel, out_shape=(jax.ShapeDtypeStruct((1, 2 * STEPS), F3...]
    unnamed x12 -> x2, local copies, waits for them, and re-layouts: 6.34 us -> 2.75 us
where the time goes in v2:
time: 172 us
  Pallas kernels  165 us (96%)
  local copies, waits for them, and re-layouts  3.52 us (2%)
  other arithmetic  2.05 us (1%)
    pallas_call x1, Pallas kernels, local(): pl.pallas_call(kernel, out_shape=(jax.ShapeDtypeStruct((1, 2 * STEPS), F3...  165 us

profile of v2, /device:TPU:8, one launch (start us, length us, event | category | flops | bytes accessed | tf_op | source)
XLA Modules:
  0.0 171.5 jit_solution(797407368824355542)
XLA Ops:
  0.6 0.8 lt.32
  1.4 0.2 convert_reduce_fusion
  1.6 0.7 select_reduce_fusion
  2.3 0.6 convert_reduce_fusion.1
  2.9 0.5 add_maximum_fusion.last_hbm
  3.4 165.3 %lanczos.1 = (f32[1,6]{1,0:T(1,128)}, f32[4,128,128]{2,1,0:T(8,128)}) custom-call(bf16[4,128,128]{2,1,0:T(8,128)(2,1)} %bitcast.10, bf16[4,34,128,128]{3,2,1,0:T(8,128)(2,1)} %bitcast.8, bf16[136,128,128]{2,1,0:T(8,128)(2,1)} %bitcast.9, f32[4]{0:T(128)} %bitcast.11, s32[4]{0:T(128)} %bitcast.12, s32[4]{0:T(128)} %bitcast.13, ...), custom_call_target="tpu_custom_call" | custom-call | flops 3422552064 | bytes 8912896 | tf_op jit(solution)/shard_map/lanczos/pallas_call | solution.py:584
  168.8 1.1 copy.11
  169.8 1.7 copy.12

commit v3 on v2

--- a/solution.py
+++ b/solution.py
@@ -20,6 +20,7 @@
 PR = 32
 NP = T // PR
 HR = PR // 2
+NX = 14
 NA = (2, 2, 1, 1)
 A2_DIRECT = (True,) * NP
 B2_ROUNDS = (2, 2, 2, 2)
@@ -69,6 +70,9 @@
     xz,
     lt_send,
     lt_recv,
+    round_box,
+    round_send,
+    round_recv,
     rt_sem,
     a1_send,
     a1_recv,
@@ -98,6 +102,17 @@
     peers += [at(dz=d) for d in (4, 3, 5, 2, 6, 1, 7)] + [at(dy=d) for d in (2, 1, 3)]
     for peer in peers:
         pl.semaphore_signal(barrier, inc=1, device_id=peer, device_id_type=MESH)
+    odd = lax.rem(seg, 2)
+
+    @pl.when(odd == 1)
+    def _():
+        for ds in (2, -2, -3):
+            pl.semaphore_signal(barrier, inc=1, device_id=at(ds=ds), device_id_type=MESH)
+
+    @pl.when(odd == 0)
+    def _():
+        pl.semaphore_signal(barrier, inc=1, device_id=at(ds=3), device_id_type=MESH)
+
     energy_ref, rows_ref, cols_ref, order_ref, goal_ref, last_ref, has_ref = scalars
     local_copies = [pltpu.make_async_copy(start_hbm, start_ref, scalar_sem.at[7])]
     sources = (energy_hbm, rows_hbm, cols_hbm, order_hbm, goal_hbm, last_hbm, has_hbm)
@@ -106,21 +121,52 @@
     local_copies.append(pltpu.make_async_copy(right_ref, rt, rt_sem))
     for copy in local_copies:
         copy.start()
-    pl.semaphore_wait(barrier, len(peers))
+    pl.semaphore_wait(barrier, len(peers) + 1 + 2 * odd)
 
     def lt_copy(j, k):
+        tile = min(k, NK - 1)
+        first, count = ((0, NW), (0, NW - NX), (NW - NX, NX))[max(k - NK + 2, 0)]
         return pltpu.make_async_remote_copy(
-            src_ref=left_ref.at[k, :, pl.ds(j * PR, PR), :],
-            dst_ref=lt.at[j, pl.ds(k * NW, NW)],
+            src_ref=left_ref.at[tile, pl.ds(first, count), pl.ds(j * PR, PR), :],
+            dst_ref=lt.at[j, pl.ds(tile * NW + first, count)],
             send_sem=lt_send.at[j, k],
             recv_sem=lt_recv.at[j, k],
             device_id=at(ds=1),
             device_id_type=MESH,
         )
 
-    for j in range(NP):
+    def round_copy(j, hop):
+        source = left_ref.at[NK - 1, pl.ds(NW - NX, NX), pl.ds(j * PR, PR), :]
+        return pltpu.make_async_remote_copy(
+            src_ref=source if hop == 0 else round_box.at[hop - 1, j],
+            dst_ref=lt.at[j, pl.ds(NS - NX, NX)] if hop == 2 else round_box.at[hop, j],
+            send_sem=round_send.at[hop, j],
+            recv_sem=lt_recv.at[j, NK] if hop == 2 else round_recv.at[hop, j],
+            device_id=at(ds=-3) if hop == 2 else at(ds=-2),
+            device_id_type=MESH,
+        )
+
+    def pass_round(*moves):
+        @pl.when(odd == 1)
+        def _():
+            for j, hop in moves:
+                round_copy(j, hop - 1).wait_recv()
+                round_copy(j, hop).start()
+
+    def send_piece(j):
         for k in range(NK):
             lt_copy(j, k).start()
+
+        @pl.when(odd == 0)
+        def _():
+            lt_copy(j, NK).start()
+
+    @pl.when(odd == 1)
+    def _():
+        for j in range(NP):
+            round_copy(j, 0).start()
+
+    send_piece(0)
     for copy in local_copies:
         copy.wait()
 
@@ -197,7 +243,10 @@
         squares.append(q * q)
     weighted = total([square * energy_ref[i] for i, square in enumerate(squares)])
     exchange_open(STEPS, [zero, total(squares), zero, zero, weighted, zero, zero])
+    pass_round((0, 1))
     exchange_pass(STEPS)
+    send_piece(1)
+    pass_round((1, 1))
     _, size, _, _, weighted, _, _ = exchange_close(STEPS)
     scale = lax.rsqrt(size / ENTRIES + EPS)
     shift = mean_energy(weighted, size)
@@ -209,6 +258,8 @@
         near[i] = jnp.zeros((T, T), F32)
         low[i] = (q * feeds_left).astype(BF16)
     coef[...] = jnp.zeros((1, T), F32)
+    pass_round((2, 1), (0, 2), (3, 1), (1, 2))
+    send_piece(2)
 
     def ring(side, bufs, boxes, sends, recvs, n, me, move):
         far = n // 2
@@ -516,11 +567,14 @@
     for j in range(NP):
         for i in range(j):
             play(i, 2 * (j - i) - 1)
-        for k in range(NK):
+        for k in range(NK + 1):
             lt_copy(j, k).wait_recv()
         contributions(j, 1)
         for i in range(j + 1):
             play(i, 2 * (j - i))
+        if j == 0:
+            pass_round((2, 2), (3, 2))
+            send_piece(3)
     for turn in range(1, turns):
         for j in range(NP):
             play(j, 2 * (NP - 1 - j) + turn)
@@ -528,6 +582,16 @@
     for j in range(NP):
         for k in range(NK):
             lt_copy(j, k).wait_send()
+
+        @pl.when(odd == 1)
+        def _():
+            for hop in range(3):
+                round_copy(j, hop).wait_send()
+
+        @pl.when(odd == 0)
+        def _():
+            lt_copy(j, NK).wait_send()
+
     settle(None, None, zero, shift)
 
     for n in range(1, STEPS):
@@ -616,8 +680,11 @@
             pltpu.VMEM((STEPS + 1, 2, 8, T), F32),
             pltpu.VMEM((STEPS + 1, NY, 8, T), F32),
             pltpu.VMEM((STEPS + 1, NZ, 8, T), F32),
-            dma((NP, NK)),
-            dma((NP, NK)),
+            dma((NP, NK + 1)),
+            dma((NP, NK + 1)),
+            pltpu.VMEM((2, NP, NX, PR, T), BF16),
+            dma((3, NP)),
+            dma((3, NP)),
             dma,
             dma((2 * NP, 2, NZ // 2)),
             dma((2 * NP, 2, NZ // 2)),

time: 172 us -> 166 us (0.965)
  Pallas kernels: 165 us -> 160 us
    pallas_call x1, Pallas kernels: 165 us -> 160 us  [local(): pl.pallas_call(kernel, out_shape=(jax.ShapeDtypeStruct((1, 2 * STEPS), F3...]
where the time goes in v3:
time: 166 us
  Pallas kernels  160 us (96%)
  local copies, waits for them, and re-layouts  3.52 us (2%)
  other arithmetic  2.05 us (1%)
    pallas_call x1, Pallas kernels, local(): pl.pallas_call(kernel, out_shape=(jax.ShapeDtypeStruct((1, 2 * STEPS), F3...  160 us

profile of v3, /device:TPU:8, one launch (start us, length us, event | category | flops | bytes accessed | tf_op | source)
XLA Modules:
  0.0 165.9 jit_solution(1182122816156437661)
XLA Ops:
  0.6 0.8 lt.32
  1.4 0.2 convert_reduce_fusion
  1.6 0.7 select_reduce_fusion
  2.3 0.6 convert_reduce_fusion.1
  2.9 0.5 add_maximum_fusion.last_hbm
  3.4 159.7 %lanczos.1 = (f32[1,6]{1,0:T(1,128)}, f32[4,128,128]{2,1,0:T(8,128)}) custom-call(bf16[4,128,128]{2,1,0:T(8,128)(2,1)} %bitcast.10, bf16[4,34,128,128]{3,2,1,0:T(8,128)(2,1)} %bitcast.8, bf16[136,128,128]{2,1,0:T(8,128)(2,1)} %bitcast.9, f32[4]{0:T(128)} %bitcast.11, s32[4]{0:T(128)} %bitcast.12, s32[4]{0:T(128)} %bitcast.13, ...), custom_call_target="tpu_custom_call" | custom-call | flops 3422552064 | bytes 8912896 | tf_op jit(solution)/shard_map/lanczos/pallas_call | solution.py:648
  163.2 1.1 copy.11
  164.3 1.7 %copy.12 = f32[1,4,128,128]{3,2,1,0:T(8,128)} copy(f32[1,4,128,128]{3,2,1,0:T(8,128)} %bitcast.7) | data formatting | bytes 524288

commit v4 on v3

--- a/solution.py
+++ b/solution.py
@@ -468,7 +468,7 @@
     networks = [network(0), network(1)]
 
     CH = 17
-    UN = 8
+    UN = 17
 
     def contributions(first, count):
         rows = count * PR

time: 166 us -> 164 us (0.988)
  Pallas kernels: 160 us -> 157 us
    pallas_call x1, Pallas kernels: 160 us -> 157 us  [local(): pl.pallas_call(kernel, out_shape=(jax.ShapeDtypeStruct((1, 2 * STEPS), F3...]
where the time goes in v4:
time: 164 us; the launch traced here: 163 us
  Pallas kernels  157 us (96%)
  local copies, waits for them, and re-layouts  3.52 us (2%)
  other arithmetic  2.05 us (1%)
    pallas_call x1, Pallas kernels, local(): pl.pallas_call(kernel, out_shape=(jax.ShapeDtypeStruct((1, 2 * STEPS), F3...  157 us

profile of v4, /device:TPU:8, one launch (start us, length us, event | category | flops | bytes accessed | tf_op | source)
XLA Modules:
  0.0 163.2 jit_solution(14732894110510770690)
XLA Ops:
  0.6 0.8 lt.32
  1.4 0.2 convert_reduce_fusion
  1.6 0.7 select_reduce_fusion
  2.3 0.6 convert_reduce_fusion.1
  2.9 0.5 add_maximum_fusion.last_hbm
  3.4 157.0 %lanczos.1 = (f32[1,6]{1,0:T(1,128)}, f32[4,128,128]{2,1,0:T(8,128)}) custom-call(bf16[4,128,128]{2,1,0:T(8,128)(2,1)} %bitcast.10, bf16[4,34,128,128]{3,2,1,0:T(8,128)(2,1)} %bitcast.8, bf16[136,128,128]{2,1,0:T(8,128)(2,1)} %bitcast.9, f32[4]{0:T(128)} %bitcast.11, s32[4]{0:T(128)} %bitcast.12, s32[4]{0:T(128)} %bitcast.13, ...), custom_call_target="tpu_custom_call" | custom-call | flops 3422552064 | bytes 8912896 | tf_op jit(solution)/shard_map/lanczos/pallas_call | solution.py:648
  160.5 1.1 copy.11
  161.6 1.7 %copy.12 = f32[1,4,128,128]{3,2,1,0:T(8,128)} copy(f32[1,4,128,128]{3,2,1,0:T(8,128)} %bitcast.7) | data formatting | bytes 524288
